TPU v7x, 512 devices: a whole 4x4x16 slice. The times are simulated.
512 devices in a mesh: section: 16 (over z), expert: 32 (over y, x, core).
Axes of the slice: x: 4, y: 4, z: 16, core: 2. Of those that a mesh axis runs over, the one named last changes fastest.
Arguments:
- tokens: bfloat16 [8, 256, 2048], P(None, 'expert', 'section'), may hold values from -6 to 6
- norm_gain: float32 [16, 2048], P('section'), may hold values from 0.1 to 1.9
- gate_weight: bfloat16 [16, 32, 2048, 384], P('section', 'expert'), may hold values from -0.125 to 0.125
- up_weight: bfloat16 [16, 32, 2048, 384], P('section', 'expert'), may hold values from -0.125 to 0.125
- down_weight: bfloat16 [16, 32, 384, 2048], P('section', 'expert'), may hold values from -0.3125 to 0.3125
- expert_ids: int32 [16, 8, 256, 8], P('section', None, 'expert'), may hold values from 0 to 31, all different within a row; in each aligned block of 8 rows (0 to 7, 8 to 15, ..., all dimensions but the last counted through in order) at most 2 rows name the same one
- gate_probs: float32 [16, 8, 256, 8], P('section', None, 'expert'), may hold values from 0.05 to 1
Outputs:
- hidden_states: bfloat16 [16, 8, 256, 2048], P('section', None, 'expert')
Inputs may be any that keep to these rules, and one draw needn't show every extreme that they name: `expert_ids`: in the 8 rows of one index of expert for one layer and micro-batch (aligned blocks of 8 rows), no expert is named by more than 2 rows, a bound that some block reaches in every draw.
All inputs are finite; a program needn't handle non-finite values.
Results may differ from a plain program's by a relative error of at most 0.04.
Values may be sent and summed in bfloat16 or wider, within the bound.
No kernel may reach another device: no remote copies, remote signals or barrier semaphores. Data moves between devices by JAX's collectives and lax.ppermute only.
A program may use at most 64 MiB of HBM per device.

v0:
```python
import jax
import jax.numpy as jnp
from jax import lax
from jax.sharding import PartitionSpec as P

CAP = 2
EPS = 1e-06


def passed_along(value, axis, by):
    length = lax.axis_size(axis)
    pairs = [(i, i + by) for i in range(length) if 0 <= i + by < length]
    return lax.ppermute(value, axis, pairs)


def expert_block(routed, w_gate, w_up, w_down):
    gate_proj = jnp.einsum("escd,edf->escf", routed, w_gate, preferred_element_type=jnp.float32)
    up_proj = jnp.einsum("escd,edf->escf", routed, w_up, preferred_element_type=jnp.float32)
    active = (jax.nn.silu(gate_proj) * up_proj).astype(jnp.bfloat16)
    return jnp.einsum("escf,efd->escd", active, w_down, preferred_element_type=jnp.float32).astype(
        jnp.bfloat16
    )


def slot_numbers(flat_ids, experts, capacity):
    onehot = (flat_ids[..., None] == jnp.arange(experts, dtype=jnp.int32)).astype(jnp.int32)
    before = jnp.cumsum(onehot, axis=-2) - onehot
    return flat_ids * capacity + jnp.sum(onehot * before, axis=-1)


def moe_layer(layer_input, norm_scale, expert_list, gate_share, w_gate, w_up, w_down):
    row_count, columns = layer_input.shape
    top_count = expert_list.shape[1]
    experts_local = w_gate.shape[0]
    groups = lax.axis_size("expert")
    experts = experts_local * groups
    capacity = CAP
    widened = layer_input.astype(jnp.float32)
    normed = (
        widened * lax.rsqrt(jnp.mean(widened * widened, axis=-1, keepdims=True) + EPS) * norm_scale
    ).astype(jnp.bfloat16)
    weight = gate_share / jnp.sum(gate_share, axis=-1, keepdims=True)
    slot_index = slot_numbers(
        expert_list.reshape(row_count * top_count), experts, capacity
    ).reshape(row_count, top_count)
    target = jnp.arange(experts * capacity, dtype=jnp.int32)
    placement = jnp.sum(
        (slot_index[None, :, :] == target[:, None, None]).astype(jnp.bfloat16), axis=2
    )
    sending = jnp.dot(placement, normed, preferred_element_type=jnp.float32).astype(jnp.bfloat16)
    sending = sending.reshape(experts, 1, capacity, columns)
    results = expert_block(
        lax.all_to_all(sending, "expert", split_axis=0, concat_axis=1, tiled=True),
        w_gate,
        w_up,
        w_down,
    )
    returned = lax.all_to_all(results, "expert", split_axis=1, concat_axis=0, tiled=True)
    returns_wide = returned.reshape(experts * capacity, columns).astype(jnp.float32)
    mixing = jnp.sum(
        (slot_index[:, :, None] == target[None, None, :]).astype(jnp.float32) * weight[:, :, None],
        axis=1,
    )
    mixed = jnp.dot(mixing, returns_wide, precision=lax.Precision.HIGHEST)
    return (widened + mixed).astype(jnp.bfloat16)


def local(tokens, norm_gain, gate_weight, up_weight, down_weight, expert_ids, gate_probs):
    section_index = lax.axis_index("section")
    section_count = lax.axis_size("section")
    full_tokens = lax.all_gather(tokens, "section", axis=2, tiled=True)
    micro_count, row_count, columns = full_tokens.shape
    turn_count = section_count + micro_count - 1
    norm_scale = norm_gain[0]
    w_gate = gate_weight[0]
    w_up = up_weight[0]
    w_down = down_weight[0]
    layer_ids = expert_ids[0]
    layer_probs = gate_probs[0]

    def advance(turn_index, state_pair):
        incoming, hidden_out = state_pair
        micro_index = turn_index - section_index
        is_valid = (micro_index >= 0) & (micro_index < micro_count)
        micro_pick = jnp.clip(micro_index, 0, micro_count - 1)
        fresh_rows = lax.dynamic_index_in_dim(full_tokens, micro_pick, 0, keepdims=False)
        layer_input = jnp.where(section_index == 0, fresh_rows, incoming)
        expert_list = lax.dynamic_index_in_dim(layer_ids, micro_pick, 0, keepdims=False)
        gate_share = lax.dynamic_index_in_dim(layer_probs, micro_pick, 0, keepdims=False)
        layer_output = moe_layer(
            layer_input, norm_scale, expert_list, gate_share, w_gate, w_up, w_down
        )
        updated = lax.dynamic_update_index_in_dim(hidden_out, layer_output, micro_pick, 0)
        hidden_out = jnp.where(is_valid, updated, hidden_out)
        passed = passed_along(layer_output, "section", 1)
        return (passed, hidden_out)

    initial = (
        jnp.zeros((row_count, columns), jnp.bfloat16),
        jnp.zeros((micro_count, row_count, columns), jnp.bfloat16),
    )
    final_pair = lax.fori_loop(0, turn_count, advance, initial)
    return final_pair[1][None]


def solution(mesh):
    in_specs = (
        P(None, "expert", "section"),
        P("section", None),
        P("section", "expert", None, None),
        P("section", "expert", None, None),
        P("section", "expert", None, None),
        P("section", None, "expert", None),
        P("section", None, "expert", None),
    )
    out_specs = P("section", None, "expert", None)
    return jax.shard_map(local, mesh=mesh, in_specs=in_specs, out_specs=out_specs, check_vma=False)
```

profile of v0, /device:TPU:128, one launch (start us, length us, event | category | flops | bytes accessed | tf_op | source)
XLA Modules:
  0.0 1059.5 jit_solution(3199038238281607523)
XLA Ops:
  0.0 33.5 %all_gather.3 = bf16[8,8,2048]{2,1,0:T(8,128)(2,1)} all-gather(bf16[8,8,128]{2,1,0:T(8,128)(2,1)} %param.9), channel_id=1, replica_groups=mesh['section'=16,'expert'=32] {'section'}, dimensions={2}, use_global_device_ids=true | all-gather | bytes 278528 | tf_op jit(solution)/shard_map/all_gather | solution.py:71
  34.2 1025.2 %while.17 = (s32[]{:T(128)}, bf16[8,2048]{1,0:T(8,128)(2,1)S(1)}, bf16[8,8,2048]{2,1,0:T(8,128)(2,1)}, pred[]{:T(512)}, s32[]{:T(128)}, /*index=5*/bf16[8,8,2048...) while((s32[]{:T(128)}, bf16[8,2048]{1,0:T(8,128)(2,1)S(1)}, ...), condition=%wide.region_7.8_spmd, body=%wide.region_0.7_spmd.sunk | while | flops 317443392 | bytes 22401360 | solution.py:102
  65.3 8.0 all-to-all-done.1
  109.8 8.0 all-to-all-done.1
  154.2 8.0 all-to-all-done.1
  198.6 8.0 all-to-all-done.1
  243.0 8.0 all-to-all-done.1
  287.5 8.0 all-to-all-done.1
  331.9 8.0 all-to-all-done.1
  376.3 8.0 all-to-all-done.1
  420.7 8.0 all-to-all-done.1
  465.2 8.0 all-to-all-done.1
  509.6 8.0 all-to-all-done.1
  554.0 8.0 all-to-all-done.1
  598.4 8.0 all-to-all-done.1
  687.3 8.0 all-to-all-done.1
  731.7 8.0 all-to-all-done.1
  776.1 8.0 all-to-all-done.1
  820.6 8.0 all-to-all-done.1
  865.0 8.0 all-to-all-done.1
  909.4 8.0 all-to-all-done.1
  953.9 8.0 all-to-all-done.1
  998.3 8.0 all-to-all-done.1
  1042.7 8.0 all-to-all-done.1
  (716 shorter events, 846.9 us)
Async XLA Ops:
  39.1 16.2 %all-to-all-start = ((bf16[32,1,2,2048]{3,2,1,0:T(2,128)(2,1)}), bf16[32,1,2,2048]{3,2,1,0:T(2,128)(2,1)S(1)}, u32[]{:S(2)}, u32[]{:S(2)}) async-start(bf16[32,1,2,2048]{3,2,1,0:T(2,128)(2,1)} %bitcast.85), calls=%async_computation | async-start | bytes 524288 | tf_op jit(solution)/shard_map/while/body/eval_jaxpr/all_to_all | solution.py:53
  87.0 12.8 %all-to-all-start = ((bf16[32,1,2,2048]{3,2,1,0:T(2,128)(2,1)}), bf16[32,1,2,2048]{3,2,1,0:T(2,128)(2,1)S(1)}, u32[]{:S(2)}, u32[]{:S(2)}) async-start(bf16[32,1,2,2048]{3,2,1,0:T(2,128)(2,1)} %bitcast.85), calls=%async_computation | async-start | bytes 524288 | tf_op jit(solution)/shard_map/while/body/eval_jaxpr/all_to_all | solution.py:53
  105.0 12.8 %all-to-all-start.1 = ((bf16[1,32,2,2048]{3,2,0,1:T(2,128)(2,1)}), bf16[1,32,2,2048]{3,2,0,1:T(2,128)(2,1)S(1)}, u32[]{:S(2)}, u32[]{:S(2)}) async-start(bf16[1,32,2,2048]{3,2,0,1:T(2,128)(2,1)} %copy.31), calls=%async_computation.1 | async-start | bytes 524288 | tf_op jit(solution)/shard_map/while/body/eval_jaxpr/all_to_all | solution.py:58
  131.4 12.8 %all-to-all-start = ((bf16[32,1,2,2048]{3,2,1,0:T(2,128)(2,1)}), bf16[32,1,2,2048]{3,2,1,0:T(2,128)(2,1)S(1)}, u32[]{:S(2)}, u32[]{:S(2)}) async-start(bf16[32,1,2,2048]{3,2,1,0:T(2,128)(2,1)} %bitcast.85), calls=%async_computation | async-start | bytes 524288 | tf_op jit(solution)/shard_map/while/body/eval_jaxpr/all_to_all | solution.py:53
  175.9 12.8 %all-to-all-start = ((bf16[32,1,2,2048]{3,2,1,0:T(2,128)(2,1)}), bf16[32,1,2,2048]{3,2,1,0:T(2,128)(2,1)S(1)}, u32[]{:S(2)}, u32[]{:S(2)}) async-start(bf16[32,1,2,2048]{3,2,1,0:T(2,128)(2,1)} %bitcast.85), calls=%async_computation | async-start | bytes 524288 | tf_op jit(solution)/shard_map/while/body/eval_jaxpr/all_to_all | solution.py:53
  220.3 12.8 %all-to-all-start = ((bf16[32,1,2,2048]{3,2,1,0:T(2,128)(2,1)}), bf16[32,1,2,2048]{3,2,1,0:T(2,128)(2,1)S(1)}, u32[]{:S(2)}, u32[]{:S(2)}) async-start(bf16[32,1,2,2048]{3,2,1,0:T(2,128)(2,1)} %bitcast.85), calls=%async_computation | async-start | bytes 524288 | tf_op jit(solution)/shard_map/while/body/eval_jaxpr/all_to_all | solution.py:53
  264.7 12.8 %all-to-all-start = ((bf16[32,1,2,2048]{3,2,1,0:T(2,128)(2,1)}), bf16[32,1,2,2048]{3,2,1,0:T(2,128)(2,1)S(1)}, u32[]{:S(2)}, u32[]{:S(2)}) async-start(bf16[32,1,2,2048]{3,2,1,0:T(2,128)(2,1)} %bitcast.85), calls=%async_computation | async-start | bytes 524288 | tf_op jit(solution)/shard_map/while/body/eval_jaxpr/all_to_all | solution.py:53
  309.1 12.8 %all-to-all-start = ((bf16[32,1,2,2048]{3,2,1,0:T(2,128)(2,1)}), bf16[32,1,2,2048]{3,2,1,0:T(2,128)(2,1)S(1)}, u32[]{:S(2)}, u32[]{:S(2)}) async-start(bf16[32,1,2,2048]{3,2,1,0:T(2,128)(2,1)} %bitcast.85), calls=%async_computation | async-start | bytes 524288 | tf_op jit(solution)/shard_map/while/body/eval_jaxpr/all_to_all | solution.py:53
  353.6 12.8 %all-to-all-start = ((bf16[32,1,2,2048]{3,2,1,0:T(2,128)(2,1)}), bf16[32,1,2,2048]{3,2,1,0:T(2,128)(2,1)S(1)}, u32[]{:S(2)}, u32[]{:S(2)}) async-start(bf16[32,1,2,2048]{3,2,1,0:T(2,128)(2,1)} %bitcast.85), calls=%async_computation | async-start | bytes 524288 | tf_op jit(solution)/shard_map/while/body/eval_jaxpr/all_to_all | solution.py:53
  398.0 12.8 %all-to-all-start = ((bf16[32,1,2,2048]{3,2,1,0:T(2,128)(2,1)}), bf16[32,1,2,2048]{3,2,1,0:T(2,128)(2,1)S(1)}, u32[]{:S(2)}, u32[]{:S(2)}) async-start(bf16[32,1,2,2048]{3,2,1,0:T(2,128)(2,1)} %bitcast.85), calls=%async_computation | async-start | bytes 524288 | tf_op jit(solution)/shard_map/while/body/eval_jaxpr/all_to_all | solution.py:53
  442.4 12.8 %all-to-all-start = ((bf16[32,1,2,2048]{3,2,1,0:T(2,128)(2,1)}), bf16[32,1,2,2048]{3,2,1,0:T(2,128)(2,1)S(1)}, u32[]{:S(2)}, u32[]{:S(2)}) async-start(bf16[32,1,2,2048]{3,2,1,0:T(2,128)(2,1)} %bitcast.85), calls=%async_computation | async-start | bytes 524288 | tf_op jit(solution)/shard_map/while/body/eval_jaxpr/all_to_all | solution.py:53
  486.8 12.8 %all-to-all-start = ((bf16[32,1,2,2048]{3,2,1,0:T(2,128)(2,1)}), bf16[32,1,2,2048]{3,2,1,0:T(2,128)(2,1)S(1)}, u32[]{:S(2)}, u32[]{:S(2)}) async-start(bf16[32,1,2,2048]{3,2,1,0:T(2,128)(2,1)} %bitcast.85), calls=%async_computation | async-start | bytes 524288 | tf_op jit(solution)/shard_map/while/body/eval_jaxpr/all_to_all | solution.py:53
  531.3 12.8 %all-to-all-start = ((bf16[32,1,2,2048]{3,2,1,0:T(2,128)(2,1)}), bf16[32,1,2,2048]{3,2,1,0:T(2,128)(2,1)S(1)}, u32[]{:S(2)}, u32[]{:S(2)}) async-start(bf16[32,1,2,2048]{3,2,1,0:T(2,128)(2,1)} %bitcast.85), calls=%async_computation | async-start | bytes 524288 | tf_op jit(solution)/shard_map/while/body/eval_jaxpr/all_to_all | solution.py:53
  575.7 12.8 %all-to-all-start = ((bf16[32,1,2,2048]{3,2,1,0:T(2,128)(2,1)}), bf16[32,1,2,2048]{3,2,1,0:T(2,128)(2,1)S(1)}, u32[]{:S(2)}, u32[]{:S(2)}) async-start(bf16[32,1,2,2048]{3,2,1,0:T(2,128)(2,1)} %bitcast.85), calls=%async_computation | async-start | bytes 524288 | tf_op jit(solution)/shard_map/while/body/eval_jaxpr/all_to_all | solution.py:53
  620.1 12.8 %all-to-all-start = ((bf16[32,1,2,2048]{3,2,1,0:T(2,128)(2,1)}), bf16[32,1,2,2048]{3,2,1,0:T(2,128)(2,1)S(1)}, u32[]{:S(2)}, u32[]{:S(2)}) async-start(bf16[32,1,2,2048]{3,2,1,0:T(2,128)(2,1)} %bitcast.85), calls=%async_computation | async-start | bytes 524288 | tf_op jit(solution)/shard_map/while/body/eval_jaxpr/all_to_all | solution.py:53
  664.5 12.8 %all-to-all-start = ((bf16[32,1,2,2048]{3,2,1,0:T(2,128)(2,1)}), bf16[32,1,2,2048]{3,2,1,0:T(2,128)(2,1)S(1)}, u32[]{:S(2)}, u32[]{:S(2)}) async-start(bf16[32,1,2,2048]{3,2,1,0:T(2,128)(2,1)} %bitcast.85), calls=%async_computation | async-start | bytes 524288 | tf_op jit(solution)/shard_map/while/body/eval_jaxpr/all_to_all | solution.py:53
  709.0 12.8 %all-to-all-start = ((bf16[32,1,2,2048]{3,2,1,0:T(2,128)(2,1)}), bf16[32,1,2,2048]{3,2,1,0:T(2,128)(2,1)S(1)}, u32[]{:S(2)}, u32[]{:S(2)}) async-start(bf16[32,1,2,2048]{3,2,1,0:T(2,128)(2,1)} %bitcast.85), calls=%async_computation | async-start | bytes 524288 | tf_op jit(solution)/shard_map/while/body/eval_jaxpr/all_to_all | solution.py:53
  753.4 12.8 %all-to-all-start = ((bf16[32,1,2,2048]{3,2,1,0:T(2,128)(2,1)}), bf16[32,1,2,2048]{3,2,1,0:T(2,128)(2,1)S(1)}, u32[]{:S(2)}, u32[]{:S(2)}) async-start(bf16[32,1,2,2048]{3,2,1,0:T(2,128)(2,1)} %bitcast.85), calls=%async_computation | async-start | bytes 524288 | tf_op jit(solution)/shard_map/while/body/eval_jaxpr/all_to_all | solution.py:53
  797.8 12.8 %all-to-all-start = ((bf16[32,1,2,2048]{3,2,1,0:T(2,128)(2,1)}), bf16[32,1,2,2048]{3,2,1,0:T(2,128)(2,1)S(1)}, u32[]{:S(2)}, u32[]{:S(2)}) async-start(bf16[32,1,2,2048]{3,2,1,0:T(2,128)(2,1)} %bitcast.85), calls=%async_computation | async-start | bytes 524288 | tf_op jit(solution)/shard_map/while/body/eval_jaxpr/all_to_all | solution.py:53
  842.2 12.8 %all-to-all-start = ((bf16[32,1,2,2048]{3,2,1,0:T(2,128)(2,1)}), bf16[32,1,2,2048]{3,2,1,0:T(2,128)(2,1)S(1)}, u32[]{:S(2)}, u32[]{:S(2)}) async-start(bf16[32,1,2,2048]{3,2,1,0:T(2,128)(2,1)} %bitcast.85), calls=%async_computation | async-start | bytes 524288 | tf_op jit(solution)/shard_map/while/body/eval_jaxpr/all_to_all | solution.py:53
  886.7 12.8 %all-to-all-start = ((bf16[32,1,2,2048]{3,2,1,0:T(2,128)(2,1)}), bf16[32,1,2,2048]{3,2,1,0:T(2,128)(2,1)S(1)}, u32[]{:S(2)}, u32[]{:S(2)}) async-start(bf16[32,1,2,2048]{3,2,1,0:T(2,128)(2,1)} %bitcast.85), calls=%async_computation | async-start | bytes 524288 | tf_op jit(solution)/shard_map/while/body/eval_jaxpr/all_to_all | solution.py:53
  931.1 12.8 %all-to-all-start = ((bf16[32,1,2,2048]{3,2,1,0:T(2,128)(2,1)}), bf16[32,1,2,2048]{3,2,1,0:T(2,128)(2,1)S(1)}, u32[]{:S(2)}, u32[]{:S(2)}) async-start(bf16[32,1,2,2048]{3,2,1,0:T(2,128)(2,1)} %bitcast.85), calls=%async_computation | async-start | bytes 524288 | tf_op jit(solution)/shard_map/while/body/eval_jaxpr/all_to_all | solution.py:53
  975.5 12.8 %all-to-all-start = ((bf16[32,1,2,2048]{3,2,1,0:T(2,128)(2,1)}), bf16[32,1,2,2048]{3,2,1,0:T(2,128)(2,1)S(1)}, u32[]{:S(2)}, u32[]{:S(2)}) async-start(bf16[32,1,2,2048]{3,2,1,0:T(2,128)(2,1)} %bitcast.85), calls=%async_computation | async-start | bytes 524288 | tf_op jit(solution)/shard_map/while/body/eval_jaxpr/all_to_all | solution.py:53
  1019.9 12.8 %all-to-all-start = ((bf16[32,1,2,2048]{3,2,1,0:T(2,128)(2,1)}), bf16[32,1,2,2048]{3,2,1,0:T(2,128)(2,1)S(1)}, u32[]{:S(2)}, u32[]{:S(2)}) async-start(bf16[32,1,2,2048]{3,2,1,0:T(2,128)(2,1)} %bitcast.85), calls=%async_computation | async-start | bytes 524288 | tf_op jit(solution)/shard_map/while/body/eval_jaxpr/all_to_all | solution.py:53
  (91 other events, 1185.4 us)
where the time goes:
time: 1070 us; the launch traced here: 1060 us
  waiting for transfers between devices  469 us (44%)
  starting transfers between devices  226 us (21%)
  matrix products  138 us (13%)
  other arithmetic  102 us (10%)
  local copies, waits for them, and re-layouts  89 us (8%)
  blocking collectives  33.5 us (3%)
    all_to_all x23, waiting for transfers between devices, moe_layer(): lax.all_to_all(results, 'expert', split_axis=1, concat_axis=0, tiled=True)  185 us
    all_to_all x23, waiting for transfers between devices, moe_layer(): lax.all_to_all(sending, 'expert', split_axis=0, concat_axis=1, tiled=True)  168 us
    ppermute x23, waiting for transfers between devices, passed_along(): return lax.ppermute(value, axis, pairs)  116 us
    all_to_all x23, starting transfers between devices, moe_layer(): lax.all_to_all(sending, 'expert', split_axis=0, concat_axis=1, tiled=True)  92.5 us
    all_to_all x23, starting transfers between devices, moe_layer(): lax.all_to_all(results, 'expert', split_axis=1, concat_axis=0, tiled=True)  88.9 us
    ppermute x23, starting transfers between devices, passed_along(): return lax.ppermute(value, axis, pairs)  44.7 us
    convert_element_type x23, local copies, waits for them, and re-layouts, expert_block(): jnp.einsum('escf,efd->escd', active, w_down, preferred_element_type=jnp.f...  44.2 us
    dot_general x23, matrix products, expert_block(): jnp.einsum('escd,edf->escf', routed, w_gate, preferred_element_type=jnp.f...  40.5 us
  transfers between devices with their start and end apart: 69, of which 69 were waited for; matrix products, arithmetic and copies ran while one was open for 5% of the time, Pallas kernels for 0%

commit v1 on v0

--- a/solution.py
+++ b/solution.py
@@ -68,7 +68,25 @@
 def local(tokens, norm_gain, gate_weight, up_weight, down_weight, expert_ids, gate_probs):
     section_index = lax.axis_index("section")
     section_count = lax.axis_size("section")
-    full_tokens = lax.all_gather(tokens, "section", axis=2, tiled=True)
+    peers, index, width = (lax.axis_size("section"), lax.axis_index("section"), tokens.shape[2])
+    forward = [(i_2, (i_2 + 1) % peers) for i_2 in range(peers)]
+    downward = [(i_2, (i_2 - 1) % peers) for i_2 in range(peers)]
+    full_tokens = jnp.zeros(
+        (*tokens.shape[:2], peers * width, *tokens.shape[2 + 1 :]), tokens.dtype
+    )
+    full_tokens = lax.dynamic_update_slice_in_dim(full_tokens, tokens, index * width, axis=2)
+    from_left = from_right = tokens
+    halfway = peers // 2
+    for step in range(1, halfway + 1):
+        from_left = lax.ppermute(from_left, "section", forward)
+        full_tokens = lax.dynamic_update_slice_in_dim(
+            full_tokens, from_left, (index - step) % peers * width, axis=2
+        )
+        if step < peers - halfway:
+            from_right = lax.ppermute(from_right, "section", downward)
+            full_tokens = lax.dynamic_update_slice_in_dim(
+                full_tokens, from_right, (index + step) % peers * width, axis=2
+            )
     micro_count, row_count, columns = full_tokens.shape
     turn_count = section_count + micro_count - 1
     norm_scale = norm_gain[0]

time: 1070 us -> 1090 us (1.019)
  the two profiles are of different devices: /device:TPU:128 before, /device:TPU:384 now
where the time goes in v1:
time: 1090 us; the launch traced here: 1070 us
  waiting for transfers between devices  474 us (43%)
  starting transfers between devices  277 us (25%)
  matrix products  119 us (11%)
  other arithmetic  102 us (9%)
  local copies, waits for them, and re-layouts  100 us (9%)
    all_to_all x23, waiting for transfers between devices, moe_layer(): lax.all_to_all(results, 'expert', split_axis=1, concat_axis=0, tiled=True)  185 us
    all_to_all x23, waiting for transfers between devices, moe_layer(): lax.all_to_all(sending, 'expert', split_axis=0, concat_axis=1, tiled=True)  168 us
    ppermute x23, waiting for transfers between devices, passed_along(): return lax.ppermute(value, axis, pairs)  117 us
    all_to_all x23, starting transfers between devices, moe_layer(): lax.all_to_all(sending, 'expert', split_axis=0, concat_axis=1, tiled=True)  92.4 us
    all_to_all x23, starting transfers between devices, moe_layer(): lax.all_to_all(results, 'expert', split_axis=1, concat_axis=0, tiled=True)  89 us
    convert_element_type x23, local copies, waits for them, and re-layouts, expert_block(): jnp.einsum('escf,efd->escd', active, w_down, preferred_element_type=jnp.f...  44.5 us
    ppermute x23, starting transfers between devices, passed_along(): return lax.ppermute(value, axis, pairs)  43.9 us
    dot_general x23, matrix products, expert_block(): jnp.einsum('escd,edf->escf', routed, w_gate, preferred_element_type=jnp.f...  40.6 us
  transfers between devices with their start and end apart: 84, of which 70 were waited for; matrix products, arithmetic and copies ran while one was open for 6% of the time, Pallas kernels for 0%

profile of v1, /device:TPU:384, one launch (start us, length us, event | category | flops | bytes accessed | tf_op | source)
XLA Modules:
  0.0 1073.4 jit_solution(15136219707974554994)
XLA Ops:
  67.1 1006.2 %while.17 = (s32[]{:T(128)}, bf16[8,2048]{1,0:T(8,128)(2,1)S(1)}, bf16[8,8,2048]{2,1,0:T(8,128)(2,1)}, pred[]{:T(512)}, s32[]{:T(128)}, /*index=5*/bf16[8,8,2048...) while((s32[]{:T(128)}, bf16[8,2048]{1,0:T(8,128)(2,1)S(1)}, ...), condition=%wide.region_7.8_spmd, body=%wide.region_0.7_spmd.sunk | while | flops 317443392 | bytes 16109876 | solution.py:120
  97.4 8.0 all-to-all-done.1
  141.0 8.0 all-to-all-done.1
  184.6 8.0 all-to-all-done.1
  228.2 8.0 all-to-all-done.1
  271.8 8.0 all-to-all-done.1
  315.4 8.0 all-to-all-done.1
  359.0 8.0 all-to-all-done.1
  402.6 8.0 all-to-all-done.1
  446.2 8.0 all-to-all-done.1
  489.8 8.0 all-to-all-done.1
  533.4 8.0 all-to-all-done.1
  577.0 8.0 all-to-all-done.1
  620.6 8.0 all-to-all-done.1
  664.2 8.0 all-to-all-done.1
  707.8 8.0 all-to-all-done.1
  751.4 8.0 all-to-all-done.1
  795.0 8.0 all-to-all-done.1
  838.6 8.0 all-to-all-done.1
  882.2 8.0 all-to-all-done.1
  925.8 8.0 all-to-all-done.1
  969.4 8.0 all-to-all-done.1
  1013.0 8.0 all-to-all-done.1
  1056.6 8.0 all-to-all-done.1
  (720 shorter events, 886.4 us)
Async XLA Ops:
  71.2 16.2 %all-to-all-start = ((bf16[32,1,2,2048]{3,2,1,0:T(2,128)(2,1)}), bf16[32,1,2,2048]{3,2,1,0:T(2,128)(2,1)S(1)}, u32[]{:S(2)}, u32[]{:S(2)}) async-start(bf16[32,1,2,2048]{3,2,1,0:T(2,128)(2,1)} %bitcast.85), calls=%async_computation | async-start | bytes 524288 | tf_op jit(solution)/shard_map/while/body/eval_jaxpr/all_to_all | solution.py:53
  92.7 12.8 %all-to-all-start.1 = ((bf16[1,32,2,2048]{3,2,0,1:T(2,128)(2,1)}), bf16[1,32,2,2048]{3,2,0,1:T(2,128)(2,1)S(1)}, u32[]{:S(2)}, u32[]{:S(2)}) async-start(bf16[1,32,2,2048]{3,2,0,1:T(2,128)(2,1)} %copy.31), calls=%async_computation.1 | async-start | bytes 524288 | tf_op jit(solution)/shard_map/while/body/eval_jaxpr/all_to_all | solution.py:58
  136.3 12.8 %all-to-all-start.1 = ((bf16[1,32,2,2048]{3,2,0,1:T(2,128)(2,1)}), bf16[1,32,2,2048]{3,2,0,1:T(2,128)(2,1)S(1)}, u32[]{:S(2)}, u32[]{:S(2)}) async-start(bf16[1,32,2,2048]{3,2,0,1:T(2,128)(2,1)} %copy.31), calls=%async_computation.1 | async-start | bytes 524288 | tf_op jit(solution)/shard_map/while/body/eval_jaxpr/all_to_all | solution.py:58
  179.9 12.8 %all-to-all-start.1 = ((bf16[1,32,2,2048]{3,2,0,1:T(2,128)(2,1)}), bf16[1,32,2,2048]{3,2,0,1:T(2,128)(2,1)S(1)}, u32[]{:S(2)}, u32[]{:S(2)}) async-start(bf16[1,32,2,2048]{3,2,0,1:T(2,128)(2,1)} %copy.31), calls=%async_computation.1 | async-start | bytes 524288 | tf_op jit(solution)/shard_map/while/body/eval_jaxpr/all_to_all | solution.py:58
  223.5 12.8 %all-to-all-start.1 = ((bf16[1,32,2,2048]{3,2,0,1:T(2,128)(2,1)}), bf16[1,32,2,2048]{3,2,0,1:T(2,128)(2,1)S(1)}, u32[]{:S(2)}, u32[]{:S(2)}) async-start(bf16[1,32,2,2048]{3,2,0,1:T(2,128)(2,1)} %copy.31), calls=%async_computation.1 | async-start | bytes 524288 | tf_op jit(solution)/shard_map/while/body/eval_jaxpr/all_to_all | solution.py:58
  267.1 12.8 %all-to-all-start.1 = ((bf16[1,32,2,2048]{3,2,0,1:T(2,128)(2,1)}), bf16[1,32,2,2048]{3,2,0,1:T(2,128)(2,1)S(1)}, u32[]{:S(2)}, u32[]{:S(2)}) async-start(bf16[1,32,2,2048]{3,2,0,1:T(2,128)(2,1)} %copy.31), calls=%async_computation.1 | async-start | bytes 524288 | tf_op jit(solution)/shard_map/while/body/eval_jaxpr/all_to_all | solution.py:58
  310.7 12.8 %all-to-all-start.1 = ((bf16[1,32,2,2048]{3,2,0,1:T(2,128)(2,1)}), bf16[1,32,2,2048]{3,2,0,1:T(2,128)(2,1)S(1)}, u32[]{:S(2)}, u32[]{:S(2)}) async-start(bf16[1,32,2,2048]{3,2,0,1:T(2,128)(2,1)} %copy.31), calls=%async_computation.1 | async-start | bytes 524288 | tf_op jit(solution)/shard_map/while/body/eval_jaxpr/all_to_all | solution.py:58
  354.3 12.8 %all-to-all-start.1 = ((bf16[1,32,2,2048]{3,2,0,1:T(2,128)(2,1)}), bf16[1,32,2,2048]{3,2,0,1:T(2,128)(2,1)S(1)}, u32[]{:S(2)}, u32[]{:S(2)}) async-start(bf16[1,32,2,2048]{3,2,0,1:T(2,128)(2,1)} %copy.31), calls=%async_computation.1 | async-start | bytes 524288 | tf_op jit(solution)/shard_map/while/body/eval_jaxpr/all_to_all | solution.py:58
  397.9 12.8 %all-to-all-start.1 = ((bf16[1,32,2,2048]{3,2,0,1:T(2,128)(2,1)}), bf16[1,32,2,2048]{3,2,0,1:T(2,128)(2,1)S(1)}, u32[]{:S(2)}, u32[]{:S(2)}) async-start(bf16[1,32,2,2048]{3,2,0,1:T(2,128)(2,1)} %copy.31), calls=%async_computation.1 | async-start | bytes 524288 | tf_op jit(solution)/shard_map/while/body/eval_jaxpr/all_to_all | solution.py:58
  441.5 12.8 %all-to-all-start.1 = ((bf16[1,32,2,2048]{3,2,0,1:T(2,128)(2,1)}), bf16[1,32,2,2048]{3,2,0,1:T(2,128)(2,1)S(1)}, u32[]{:S(2)}, u32[]{:S(2)}) async-start(bf16[1,32,2,2048]{3,2,0,1:T(2,128)(2,1)} %copy.31), calls=%async_computation.1 | async-start | bytes 524288 | tf_op jit(solution)/shard_map/while/body/eval_jaxpr/all_to_all | solution.py:58
  485.1 12.8 %all-to-all-start.1 = ((bf16[1,32,2,2048]{3,2,0,1:T(2,128)(2,1)}), bf16[1,32,2,2048]{3,2,0,1:T(2,128)(2,1)S(1)}, u32[]{:S(2)}, u32[]{:S(2)}) async-start(bf16[1,32,2,2048]{3,2,0,1:T(2,128)(2,1)} %copy.31), calls=%async_computation.1 | async-start | bytes 524288 | tf_op jit(solution)/shard_map/while/body/eval_jaxpr/all_to_all | solution.py:58
  528.7 12.8 %all-to-all-start.1 = ((bf16[1,32,2,2048]{3,2,0,1:T(2,128)(2,1)}), bf16[1,32,2,2048]{3,2,0,1:T(2,128)(2,1)S(1)}, u32[]{:S(2)}, u32[]{:S(2)}) async-start(bf16[1,32,2,2048]{3,2,0,1:T(2,128)(2,1)} %copy.31), calls=%async_computation.1 | async-start | bytes 524288 | tf_op jit(solution)/shard_map/while/body/eval_jaxpr/all_to_all | solution.py:58
  572.3 12.8 %all-to-all-start.1 = ((bf16[1,32,2,2048]{3,2,0,1:T(2,128)(2,1)}), bf16[1,32,2,2048]{3,2,0,1:T(2,128)(2,1)S(1)}, u32[]{:S(2)}, u32[]{:S(2)}) async-start(bf16[1,32,2,2048]{3,2,0,1:T(2,128)(2,1)} %copy.31), calls=%async_computation.1 | async-start | bytes 524288 | tf_op jit(solution)/shard_map/while/body/eval_jaxpr/all_to_all | solution.py:58
  615.9 12.8 %all-to-all-start.1 = ((bf16[1,32,2,2048]{3,2,0,1:T(2,128)(2,1)}), bf16[1,32,2,2048]{3,2,0,1:T(2,128)(2,1)S(1)}, u32[]{:S(2)}, u32[]{:S(2)}) async-start(bf16[1,32,2,2048]{3,2,0,1:T(2,128)(2,1)} %copy.31), calls=%async_computation.1 | async-start | bytes 524288 | tf_op jit(solution)/shard_map/while/body/eval_jaxpr/all_to_all | solution.py:58
  659.5 12.8 %all-to-all-start.1 = ((bf16[1,32,2,2048]{3,2,0,1:T(2,128)(2,1)}), bf16[1,32,2,2048]{3,2,0,1:T(2,128)(2,1)S(1)}, u32[]{:S(2)}, u32[]{:S(2)}) async-start(bf16[1,32,2,2048]{3,2,0,1:T(2,128)(2,1)} %copy.31), calls=%async_computation.1 | async-start | bytes 524288 | tf_op jit(solution)/shard_map/while/body/eval_jaxpr/all_to_all | solution.py:58
  703.1 12.8 %all-to-all-start.1 = ((bf16[1,32,2,2048]{3,2,0,1:T(2,128)(2,1)}), bf16[1,32,2,2048]{3,2,0,1:T(2,128)(2,1)S(1)}, u32[]{:S(2)}, u32[]{:S(2)}) async-start(bf16[1,32,2,2048]{3,2,0,1:T(2,128)(2,1)} %copy.31), calls=%async_computation.1 | async-start | bytes 524288 | tf_op jit(solution)/shard_map/while/body/eval_jaxpr/all_to_all | solution.py:58
  746.7 12.8 %all-to-all-start.1 = ((bf16[1,32,2,2048]{3,2,0,1:T(2,128)(2,1)}), bf16[1,32,2,2048]{3,2,0,1:T(2,128)(2,1)S(1)}, u32[]{:S(2)}, u32[]{:S(2)}) async-start(bf16[1,32,2,2048]{3,2,0,1:T(2,128)(2,1)} %copy.31), calls=%async_computation.1 | async-start | bytes 524288 | tf_op jit(solution)/shard_map/while/body/eval_jaxpr/all_to_all | solution.py:58
  790.3 12.8 %all-to-all-start.1 = ((bf16[1,32,2,2048]{3,2,0,1:T(2,128)(2,1)}), bf16[1,32,2,2048]{3,2,0,1:T(2,128)(2,1)S(1)}, u32[]{:S(2)}, u32[]{:S(2)}) async-start(bf16[1,32,2,2048]{3,2,0,1:T(2,128)(2,1)} %copy.31), calls=%async_computation.1 | async-start | bytes 524288 | tf_op jit(solution)/shard_map/while/body/eval_jaxpr/all_to_all | solution.py:58
  833.9 12.8 %all-to-all-start.1 = ((bf16[1,32,2,2048]{3,2,0,1:T(2,128)(2,1)}), bf16[1,32,2,2048]{3,2,0,1:T(2,128)(2,1)S(1)}, u32[]{:S(2)}, u32[]{:S(2)}) async-start(bf16[1,32,2,2048]{3,2,0,1:T(2,128)(2,1)} %copy.31), calls=%async_computation.1 | async-start | bytes 524288 | tf_op jit(solution)/shard_map/while/body/eval_jaxpr/all_to_all | solution.py:58
  877.5 12.8 %all-to-all-start.1 = ((bf16[1,32,2,2048]{3,2,0,1:T(2,128)(2,1)}), bf16[1,32,2,2048]{3,2,0,1:T(2,128)(2,1)S(1)}, u32[]{:S(2)}, u32[]{:S(2)}) async-start(bf16[1,32,2,2048]{3,2,0,1:T(2,128)(2,1)} %copy.31), calls=%async_computation.1 | async-start | bytes 524288 | tf_op jit(solution)/shard_map/while/body/eval_jaxpr/all_to_all | solution.py:58
  921.1 12.8 %all-to-all-start.1 = ((bf16[1,32,2,2048]{3,2,0,1:T(2,128)(2,1)}), bf16[1,32,2,2048]{3,2,0,1:T(2,128)(2,1)S(1)}, u32[]{:S(2)}, u32[]{:S(2)}) async-start(bf16[1,32,2,2048]{3,2,0,1:T(2,128)(2,1)} %copy.31), calls=%async_computation.1 | async-start | bytes 524288 | tf_op jit(solution)/shard_map/while/body/eval_jaxpr/all_to_all | solution.py:58
  964.7 12.8 %all-to-all-start.1 = ((bf16[1,32,2,2048]{3,2,0,1:T(2,128)(2,1)}), bf16[1,32,2,2048]{3,2,0,1:T(2,128)(2,1)S(1)}, u32[]{:S(2)}, u32[]{:S(2)}) async-start(bf16[1,32,2,2048]{3,2,0,1:T(2,128)(2,1)} %copy.31), calls=%async_computation.1 | async-start | bytes 524288 | tf_op jit(solution)/shard_map/while/body/eval_jaxpr/all_to_all | solution.py:58
  1008.3 12.8 %all-to-all-start.1 = ((bf16[1,32,2,2048]{3,2,0,1:T(2,128)(2,1)}), bf16[1,32,2,2048]{3,2,0,1:T(2,128)(2,1)S(1)}, u32[]{:S(2)}, u32[]{:S(2)}) async-start(bf16[1,32,2,2048]{3,2,0,1:T(2,128)(2,1)} %copy.31), calls=%async_computation.1 | async-start | bytes 524288 | tf_op jit(solution)/shard_map/while/body/eval_jaxpr/all_to_all | solution.py:58
  1051.9 12.8 %all-to-all-start.1 = ((bf16[1,32,2,2048]{3,2,0,1:T(2,128)(2,1)}), bf16[1,32,2,2048]{3,2,0,1:T(2,128)(2,1)S(1)}, u32[]{:S(2)}, u32[]{:S(2)}) async-start(bf16[1,32,2,2048]{3,2,0,1:T(2,128)(2,1)} %copy.31), calls=%async_computation.1 | async-start | bytes 524288 | tf_op jit(solution)/shard_map/while/body/eval_jaxpr/all_to_all | solution.py:58
  (85 other events, 1059.1 us)
